TPU v7x, 32 devices: a whole 2x2x4 slice. The times are simulated.
32 devices in a mesh: expert: 8 (over z, y), tensor: 4 (over x, core).
Axes of the slice: x: 2, y: 2, z: 4, core: 2. Of those that a mesh axis runs over, the one named last changes fastest.
Arguments:
- hidden_in: bfloat16 [4096, 4096], P(('expert', 'tensor')), may hold values from -20 to 20
- context: bfloat16 [4096, 4096], P('expert', 'tensor'), may hold values from -6 to 6
- w_out: bfloat16 [4096, 4096], P('tensor', 'expert'), may hold values from -0.09375 to 0.09375
- norm_gain: float32 [4096], replicated, may hold values from 0.25 to 1.75
- expert_ids: int32 [4096, 8], P(('expert', 'tensor')), may hold values from 0 to 31, all different within a row; in each aligned block of 128 rows (0 to 127, 128 to 255, ...) at most 36 rows name the same one
- route_weight: float32 [4096, 8], P(('expert', 'tensor')), may hold values from 0.05 to 1
- w_gate_up: bfloat16 [32, 4096, 1536], P(('expert', 'tensor')), may hold values from -0.09375 to 0.09375
- w_down: bfloat16 [32, 768, 4096], P(('expert', 'tensor')), may hold values from -0.21875 to 0.21875
Outputs:
- attended: bfloat16 [4096, 4096], P(('expert', 'tensor'))
- mixed: bfloat16 [4096, 4096], P(('expert', 'tensor'))
Inputs may be any that keep to these rules, and one draw needn't show every extreme that they name: `expert_ids`: each row names 8 different experts. Among the 128 rows of one device no expert is named more than 36 times, and in every draw some expert is named exactly 36 times by the rows of some device.
All inputs are finite; a program needn't handle non-finite values.
Results may differ from a plain program's by a relative error of at most 0.0053.
Values may be sent and summed in bfloat16 or wider, within the bound.
No kernel may reach another device: no remote copies, remote signals or barrier semaphores. Data moves between devices by JAX's collectives and lax.ppermute only.
A program may use at most 128 MiB of HBM per device.

v0:
```python
import jax
import jax.numpy as jnp
from jax import lax
from jax.sharding import PartitionSpec as P


def expert_block(received, w_gate_up, w_down):
    block_shape = received.shape
    flattened = received.reshape(-1, block_shape[-1])
    hidden_units = w_down.shape[1]
    gate_and_up = jnp.dot(flattened, w_gate_up[0], preferred_element_type=jnp.float32)
    activated = (jax.nn.silu(gate_and_up[:, :hidden_units]) * gate_and_up[:, hidden_units:]).astype(
        jnp.bfloat16
    )
    result = jnp.dot(activated, w_down[0], preferred_element_type=jnp.float32).astype(jnp.bfloat16)
    return result.reshape(block_shape)


def on_device(hidden_in, context, w_out, norm_gain, expert_ids, route_weight, w_gate_up, w_down):
    tok_count, width = hidden_in.shape
    partial_sums = jnp.dot(
        context,
        lax.all_gather(w_out, "expert", axis=1, tiled=True),
        preferred_element_type=jnp.float32,
    )
    projected = lax.psum_scatter(partial_sums, "tensor", scatter_dimension=0, tiled=True)
    residual = hidden_in.astype(jnp.float32) + projected
    attended = residual.astype(jnp.bfloat16)
    inverse = lax.rsqrt(jnp.mean(residual * residual, axis=1, keepdims=True) + 1e-06)
    normed = (residual * inverse * norm_gain[None, :]).astype(jnp.bfloat16)
    top_count = expert_ids.shape[1]
    expert_count = lax.axis_size("expert")
    tensor_count = lax.axis_size("tensor")
    experts_all = expert_count * tensor_count
    capacity = tok_count * top_count * 9 // (8 * experts_all)
    chosen = expert_ids.reshape(-1)
    onehot = (chosen[:, None] == jnp.arange(experts_all, dtype=jnp.int32)[None, :]).astype(
        jnp.int32
    )
    before = jnp.cumsum(onehot, axis=0) - onehot
    slots = jnp.sum(before * onehot, axis=1)
    target = chosen * capacity + slots
    token_index = jnp.arange(tok_count * top_count, dtype=jnp.int32) // top_count
    send_buffer = (
        jnp.zeros((experts_all * capacity, width), jnp.bfloat16).at[target].set(normed[token_index])
    )
    send_buffer = send_buffer.reshape(experts_all, capacity, width)
    outputs = expert_block(
        lax.all_to_all(send_buffer, ("expert", "tensor"), split_axis=0, concat_axis=0, tiled=True),
        w_gate_up,
        w_down,
    )
    returned = lax.all_to_all(
        outputs, ("expert", "tensor"), split_axis=0, concat_axis=0, tiled=True
    )
    returned = returned.reshape(experts_all * capacity, width)
    picked = returned[target].reshape(tok_count, top_count, width)
    moe_sum = jnp.sum(route_weight[:, :, None] * picked, axis=1)
    mixed = (residual + moe_sum).astype(jnp.bfloat16)
    return (attended, mixed)


def solution(mesh):
    in_specs = (
        P(("expert", "tensor"), None),
        P("expert", "tensor"),
        P("tensor", "expert"),
        P(),
        P(("expert", "tensor"), None),
        P(("expert", "tensor"), None),
        P(("expert", "tensor"), None, None),
        P(("expert", "tensor"), None, None),
    )
    out_specs = (P(("expert", "tensor"), None), P(("expert", "tensor"), None))
    return jax.shard_map(
        on_device, mesh=mesh, in_specs=in_specs, out_specs=out_specs, check_vma=False
    )
```

profile of v0, /device:TPU:0, one launch (start us, length us, event | category | flops | bytes accessed | tf_op | source)
XLA Modules:
  0.0 845.4 jit_solution(2146721663493801037)
XLA Ops:
  7.2 0.0 copy-start
  7.2 0.0 all-gather.2.cloned.1.call-start
  7.2 0.7 all-gather.2.cloned.1.call-update
  7.9 0.0 reduce-scatter.2.cloned.1.call-start
  8.0 130.2 %all-gather.2.cloned.1.call-done = bf16[1024,4096]{1,0:T(8,128)(2,1)} async-done(((bf16[1024,512]{1,0:T(8,128)(2,1)}), bf16[1024,4096]{1,0:T(8,128)(2,1)}) %all-gather.2.cloned.1.call-update) | async-done | bytes 8388624 | tf_op jit(solution)/shard_map/all_gather | solution.py:23
  138.2 0.0 copy-done
  138.2 10.0 %fusion.15 = f32[512,4096]{1,0:T(8,128)} fusion(bf16[512,1024]{1,0:T(8,128)(2,1)S(1)} %copy-done, bf16[1024,4096]{1,0:T(8,128)(2,1)} %all-gather.2.cloned.1.call-done), kind=kOutput, calls=%fused_computation.38 | convolution fusion | flops 4294967296 | bytes 17825792 | tf_op jit(solution)/shard_map/dot_general | solution.py:21
  148.2 0.0 copy-start.5
  148.2 0.0 copy-start.3
  148.2 0.0 copy-start.4
  148.2 0.0 reduce-scatter.2.cloned.1.call-update
  148.3 0.7 copy-done.5
  148.9 0.1 copy.13
  149.0 0.1 eq.29
  149.1 0.1 eq.25
  149.2 9.0 %reduce-window.6 = s32[32,8,128]{2,1,0:T(8,128)S(1)} reduce-window(s32[32,8,128]{2,1,0:T(8,128)S(1)} %fusion.13, s32[]{:T(128)} %constant.31.clone.1), window={size=1x1x128 pad=0_0x0_0x127_0}, to_apply=%region_1.0 | reduce-window | flops 4161536 | bytes 262148 | tf_op jit(solution)/shard_map/reduce-window
  158.2 0.1 slice.20
  158.3 0.1 copy.15
  158.5 0.1 copy.16
  158.6 0.1 copy.12
  158.7 0.1 mul.56
  158.8 0.1 broadcast_add_fusion
  159.0 59.5 %reduce-scatter.2.cloned.1.call-done = f32[128,4096]{1,0:T(8,128)} async-done(((f32[512,4096]{1,0:T(8,128)}), f32[128,4096]{1,0:T(8,128)}) %reduce-scatter.2.cloned.1.call-update) | async-done | bytes 2097168 | tf_op jit(solution)/shard_map/reduce_scatter | solution.py:26
  218.4 0.0 copy-done.3
  218.5 1.9 multiply_reduce_fusion
  220.4 0.0 copy-done.4
  220.4 1.9 multiply_convert_fusion
  222.4 7.7 gather_fusion
  230.1 18.2 %scatter_custom_fusion = bf16[1152,4096]{1,0:T(8,128)(2,1)} fusion(s32[1024]{0:T(1024)S(1)} %bitcast.36, bf16[1024,4096]{1,0:T(8,128)(2,1)} %gather_fusion, bf16[]{:T(256)} %constant.29.clone.1), kind=kCustom, calls=%fused_computation.9 | custom fusion | bytes 9437696 | tf_op jit(solution)/shard_map/scatter | solution.py:45
  248.3 13.2 %reshape.119 = bf16[32,36,4096]{2,1,0:T(8,128)(2,1)} reshape(bf16[1152,4096]{1,0:T(8,128)(2,1)} %scatter_custom_fusion) | data formatting | bytes 18874368 | tf_op jit(solution)/shard_map/reshape | solution.py:47
  261.5 233.2 %all_to_all.10 = bf16[32,36,4096]{2,1,0:T(8,128)(2,1)} all-to-all(bf16[32,36,4096]{2,1,0:T(8,128)(2,1)} %reshape.119), channel_id=1, replica_groups=mesh['expert'=8,'tensor'=4] {'expert','tensor'}, dimensions={0} | all-to-all | bytes 18874368 | tf_op jit(solution)/shard_map/all_to_all | solution.py:49
  494.7 13.3 %reshape.120 = bf16[1152,4096]{1,0:T(8,128)(2,1)} reshape(bf16[32,36,4096]{2,1,0:T(8,128)(2,1)} %all_to_all.10) | data formatting | bytes 18874368 | tf_op jit(solution)/shard_map/reshape | solution.py:9
  507.9 18.2 %fusion.1 = f32[1152,1536]{1,0:T(8,128)S(1)} fusion(bf16[1152,4096]{1,0:T(8,128)(2,1)} %reshape.120, bf16[1,4096,1536]{2,1,0:T(8,128)(2,1)} %param.14), kind=kOutput, calls=%fused_computation.6 | convolution fusion | flops 14495514624 | bytes 29097984 | tf_op jit(solution)/shard_map/dot_general | solution.py:11
  526.2 12.5 %convolution_convert_fusion = bf16[1152,4096]{1,0:T(8,128)(2,1)} fusion(bf16[1,768,4096]{2,1,0:T(8,128)(2,1)} %param.15, f32[1152,1536]{1,0:T(8,128)S(1)} %fusion.1), kind=kOutput, calls=%fused_computation.5 | convolution fusion | flops 7257784320 | bytes 22806528 | tf_op jit(solution)/shard_map/dot_general | solution.py:15
  538.7 13.1 %reshape.121 = bf16[32,36,4096]{2,1,0:T(8,128)(2,1)} reshape(bf16[1152,4096]{1,0:T(8,128)(2,1)} %convolution_convert_fusion) | data formatting | bytes 18874368 | tf_op jit(solution)/shard_map/reshape | solution.py:16
  551.9 0.0 copy-start.6
  551.9 4.3 all-to-all-start.1
  556.1 0.0 copy-done.6
  556.1 0.1 copy.11
  556.3 232.1 %all-to-all-done.1 = bf16[32,36,4096]{2,1,0:T(8,128)(2,1)} async-done(((bf16[32,36,4096]{2,1,0:T(8,128)(2,1)}), bf16[32,36,4096]{2,1,0:T(8,128)(2,1)}, u32[]{:S(2)}, u32[]{:S(2)}) %all-to-all-start.1) | async-done | bytes 9437216 | tf_op jit(solution)/shard_map/all_to_all | solution.py:53
  788.4 13.2 %reshape.122 = bf16[1152,4096]{1,0:T(8,128)(2,1)} reshape(bf16[32,36,4096]{2,1,0:T(8,128)(2,1)} %all-to-all-done.1) | data formatting | bytes 18874368 | tf_op jit(solution)/shard_map/reshape | solution.py:56
  801.6 0.0 copy-start.1
  801.6 20.0 %gather_fusion.1 = bf16[1024,4096]{1,0:T(8,128)(2,1)} fusion(bf16[1152,4096]{1,0:T(8,128)(2,1)} %reshape.122, s32[1024]{0:T(1024)S(1)} %broadcast_clamp_fusion), kind=kCustom, calls=%fused_computation.1 | custom fusion | bytes 16781312 | tf_op jit(solution)/shard_map/gather | solution.py:57
  821.6 0.0 copy-start.2
  821.6 13.3 %fusion = f32[128,4096]{1,0:T(8,128)} fusion(bf16[1024,4096]{1,0:T(8,128)(2,1)} %gather_fusion.1, f32[128,8]{1,0:T(8,128)S(1)} %copy.11), kind=kLoop, calls=%fused_computation.4 | loop fusion | flops 12058624 | bytes 10489856 | tf_op jit(solution)/shard_map/reduce_sum | solution.py:58
  835.0 0.0 copy-done.2
  835.0 3.6 add_convert_fusion
  838.6 0.0 copy-done.1
  (10 shorter events, 0.1 us)
Async XLA Ops:
  7.2 131.0 %copy-start = (bf16[512,1024]{1,0:T(8,128)(2,1)S(1)}, bf16[512,1024]{1,0:T(8,128)(2,1)}, u32[]{:S(2)}) copy-start(bf16[512,1024]{1,0:T(8,128)(2,1)} %param.9) | copy-start | bytes 3145732
  7.2 131.0 %all-gather.2.cloned.1.call-start = ((), (), s32[]{:S(2)}) async-start(), calls=%async_computation.3 | async-start | bytes 9437184 | tf_op jit(solution)/shard_map/all_gather | solution.py:23
  7.9 210.5 %reduce-scatter.2.cloned.1.call-start = ((), (), s32[]{:S(2)}) async-start(), calls=%async_computation.4 | async-start | bytes 10485760 | tf_op jit(solution)/shard_map/reduce_scatter | solution.py:26
  148.2 0.7 copy-start.5
  148.2 70.2 %copy-start.3 = (bf16[128,4096]{1,0:T(8,128)(2,1)S(1)}, bf16[128,4096]{1,0:T(8,128)(2,1)}, u32[]{:S(2)}) copy-start(bf16[128,4096]{1,0:T(8,128)(2,1)} %param.8) | copy-start | bytes 3145732
  148.2 72.2 %copy-start.4 = (f32[4096]{0:T(1024)S(1)}, f32[4096]{0:T(1024)}, u32[]{:S(2)}) copy-start(f32[4096]{0:T(1024)} %param.11) | copy-start | bytes 49156
  551.9 4.3 copy-start.6
  551.9 236.5 %all-to-all-start.1 = ((bf16[32,36,4096]{2,1,0:T(8,128)(2,1)}), bf16[32,36,4096]{2,1,0:T(8,128)(2,1)}, u32[]{:S(2)}, u32[]{:S(2)}) async-start(bf16[32,36,4096]{2,1,0:T(8,128)(2,1)} %reshape.121), calls=%async_computation.2 | async-start | bytes 20971520 | tf_op jit(solution)/shard_map/all_to_all | solution.py:53
  801.6 37.0 %copy-start.1 = (bf16[512,1024]{1,0:T(8,128)(2,1)S(1)}, bf16[512,1024]{1,0:T(8,128)(2,1)}, u32[]{:S(2)}) copy-start(bf16[512,1024]{1,0:T(8,128)(2,1)} %param.9) | copy-start | bytes 3145732
  821.6 13.3 %copy-start.2 = (f32[128,4096]{1,0:T(8,128)S(1)}, f32[128,4096]{1,0:T(8,128)}, u32[]{:S(2)}) copy-start(f32[128,4096]{1,0:T(8,128)} %reduce-scatter.2.cloned.1.call-done) | copy-start | bytes 6291460
Sparse Core Ops, SparseCore 0:
  10.1 128.0 all-gather.1
  148.4 70.0 reduce-scatter.1
where the time goes:
time: 847 us; the launch traced here: 845 us
  waiting for transfers between devices  422 us (50%)
  blocking collectives  233 us (28%)
  local copies, waits for them, and re-layouts  100 us (12%)
  matrix products  40.8 us (5%)
  other arithmetic  30 us (4%)
  between operations  14.2 us (2%)
    all_to_all x1, blocking collectives, on_device(): lax.all_to_all(send_buffer, ('expert', 'tensor'), split_axis=0, concat_ax...  233 us
    all_to_all x1, waiting for transfers between devices, on_device(): lax.all_to_all(outputs, ('expert', 'tensor'), split_axis=0, concat_axis=0...  232 us
    all_gather x1, waiting for transfers between devices, on_device(): lax.all_gather(w_out, 'expert', axis=1, tiled=True)  130 us
    reduce_scatter x1, waiting for transfers between devices, on_device(): lax.psum_scatter(partial_sums, 'tensor', scatter_dimension=0, tiled=True)  59.5 us
    gather x1, local copies, waits for them, and re-layouts, on_device(): picked = returned[target].reshape(tok_count, top_count, width)  20 us
    dot_general x1, matrix products, expert_block(): jnp.dot(flattened, w_gate_up[0], preferred_element_type=jnp.float32)  18.2 us
    scatter x1, local copies, waits for them, and re-layouts, on_device(): jnp.zeros((experts_all * capacity, width), jnp.bfloat16).at[target]  18.2 us
  transfers between devices with their start and end apart: 3, of which 3 were waited for; matrix products, arithmetic and copies ran while one was open for 1% of the time, Pallas kernels for 0%

commit v1 on v0

v1 whole, which is shorter than its diff:
```python
import jax
import jax.numpy as jnp
from jax import lax
from jax.sharding import Mesh, PartitionSpec as P

SWAP = [(0, 1), (1, 0)]


def swap(array, axis):
    return lax.ppermute(array, axis, SWAP)


def dot(a, b):
    return jnp.dot(a, b, preferred_element_type=jnp.float32)


def after(array, *others):
    return lax.optimization_barrier((array, *others))[0]


def plane_order(planes):
    order = []
    for plane in range(planes):
        hops = [s - plane for s in range(planes) if s != plane]
        order.append(sorted(hops, key=lambda hop: (abs(hop), hop * (-1) ** plane)))
    return order


class PlaneGather:
    def __init__(self, block, zi):
        self.planes = lax.axis_size("outer")
        self.order = plane_order(self.planes)
        self.zi, self.hop = zi, 0
        self.up = self.down = block
        self.came, self.blocks = {}, [block]

    def start(self):
        self.hop += 1
        hop, planes = self.hop, self.planes
        self.up = lax.ppermute(self.up, "outer", [(i, i + 1) for i in range(hop - 1, planes - 1)])
        self.down = lax.ppermute(
            self.down, "outer", [(i, i - 1) for i in range(1, planes - hop + 1)]
        )

    def finish(self, *others):
        self.up, self.down, *_ = lax.optimization_barrier((self.up, self.down, *others))
        self.came[-self.hop], self.came[self.hop] = self.up, self.down
        hops = [self.order[plane][self.hop - 1] for plane in range(self.planes)]
        chosen = None
        for hop in sorted(set(hops)):
            if chosen is None:
                chosen = self.came[hop]
            else:
                here = jnp.zeros((), bool)
                for plane in range(self.planes):
                    if hops[plane] == hop:
                        here = here | (self.zi == plane)
                chosen = jnp.where(here, self.came[hop], chosen)
        self.blocks.append(chosen)


def project(context, w_out, expert_ids, route_weight, spots, make_tables):
    zi, yi, xi, ci = spots
    planes = lax.axis_size("outer")
    rows, depth = context.shape
    tok_count = rows // 4
    columns = PlaneGather(w_out, zi)
    columns.start()
    other_rows = swap(context, "inner")
    table = jnp.concatenate([expert_ids.astype(jnp.float32), route_weight], axis=1)
    table = jnp.stack([table, swap(table, "core")])
    table = PlaneGather(jnp.stack([table, swap(table, "pair")]), zi)
    table.start()
    parts, crossing = [], []
    for step in range(planes):
        if step:
            gate = (crossing[step - 2],) if step > 1 else ()
            columns.finish(*gate)
            table.finish(columns.up)
            if step + 1 < planes:
                columns.start()
                table.start()
        if step == 0:
            both = jnp.stack([context, other_rows]).reshape(2, 2, 2, tok_count, depth)
            theirs = lax.dynamic_index_in_dim(both, 1 - ci, 2, keepdims=False).reshape(-1, depth)
            mine = lax.dynamic_index_in_dim(both, ci, 2, keepdims=False).reshape(-1, depth)
        weights = columns.blocks[step]
        sent = dot(theirs, weights).astype(jnp.bfloat16)
        kept = dot(mine, weights) + swap(sent, "core").astype(jnp.float32)
        kept = kept.reshape(2, 2, tok_count, -1)
        sent = lax.dynamic_index_in_dim(kept, 1 - xi, 1, keepdims=False).astype(jnp.bfloat16)
        crossing.append(sent)
        kept = lax.dynamic_index_in_dim(kept, xi, 1, keepdims=False)
        kept = kept + swap(sent, "pair").astype(jnp.float32)
        other = swap(kept[1].astype(jnp.bfloat16), "inner").astype(jnp.float32)
        low = jnp.where(yi == 0, kept[0], other)
        high = jnp.where(yi == 0, other, kept[0])
        parts.append(jnp.concatenate([low, high], axis=1))
    order = jnp.array(
        [
            [([0] + hops).index(target - plane) for target in range(planes)]
            for plane, hops in enumerate(plane_order(planes))
        ]
    )[zi]
    parts = jnp.stack(parts)
    projected = jnp.concatenate(
        [lax.dynamic_index_in_dim(parts, order[p], 0, keepdims=False) for p in range(planes)], axis=1
    )
    return projected, make_tables(jnp.stack(table.blocks))


def routes(expert_ids, route_weight, expert, capacity, rounds):
    devices, tok_count, _ = expert_ids.shape
    named = expert_ids == expert
    chosen = jnp.any(named, axis=2)
    weight = jnp.sum(jnp.where(named, route_weight, 0.0), axis=2)
    earlier = jnp.arange(tok_count)[:, None] < jnp.arange(tok_count)[None, :]
    slots = dot(chosen.astype(jnp.bfloat16), earlier.astype(jnp.bfloat16)).astype(jnp.int32)
    first = jnp.arange(devices) % (devices // rounds) * capacity
    row = jnp.where(chosen, slots + first[:, None], -1)
    return row.reshape(rounds, -1), weight.reshape(rounds, -1)


def routing_tables(table, spots, capacity, rounds):
    zi, yi, xi, ci = spots
    planes, tok_count, top_count = table.shape[0], table.shape[-2], table.shape[-1] // 2
    group = planes // rounds
    rows = group * 4 * capacity
    table = table.reshape(rounds, group, 4, tok_count, -1).swapaxes(1, 2)
    table = table.reshape(planes * 4, tok_count, -1)
    pick, place = [], []
    for side in range(2):
        expert = ((zi * 2 + (yi ^ side)) * 2 + xi) * 2 + ci
        row, weight = routes(
            table[..., :top_count],
            table[..., top_count:],
            expert.astype(jnp.float32),
            capacity,
            rounds,
        )
        pick.append((row[:, None, :] == jnp.arange(rows)[None, :, None]).astype(jnp.bfloat16))
        spread = jnp.where(row[:, :, None] == jnp.arange(rows), weight[:, :, None], 0.0)
        high = spread.astype(jnp.bfloat16)
        low = (spread - high.astype(jnp.float32)).astype(jnp.bfloat16)
        place += [high, low]
    place = jnp.concatenate(place, axis=2).reshape(rounds, 2, 2, group * tok_count, -1)
    return lax.optimization_barrier((*pick, place[:, :, 0], place[:, :, 1]))


def scatter_planes(pieces, zi):
    planes = lax.axis_size("outer")
    order = plane_order(planes)

    def piece(hop):
        chosen = None
        for step in range(planes - 1):
            here = [plane for plane in range(planes) if order[plane][step] == hop]
            if not here:
                continue
            if chosen is None:
                chosen = pieces[step + 1]
            else:
                at = jnp.zeros((), bool)
                for plane in here:
                    at = at | (zi == plane)
                chosen = jnp.where(at, pieces[step + 1], chosen)
        return chosen

    up = down = None
    for hop in range(planes - 1, 0, -1):
        up = piece(hop) if up is None else piece(hop) + up.astype(jnp.float32)
        down = piece(-hop) if down is None else piece(-hop) + down.astype(jnp.float32)
        up = lax.ppermute(
            up.astype(jnp.bfloat16), "outer", [(i, i + 1) for i in range(planes - hop)]
        )
        down = lax.ppermute(
            down.astype(jnp.bfloat16), "outer", [(i, i - 1) for i in range(hop, planes)]
        )
    return up.astype(jnp.float32) + down.astype(jnp.float32)


def on_device(hidden_in, context, w_out, norm_gain, expert_ids, route_weight, w_gate_up, w_down):
    tok_count, width = hidden_in.shape
    hidden_units = w_down.shape[1]
    planes = lax.axis_size("outer")
    zi, yi = lax.axis_index("outer"), lax.axis_index("inner")
    xi, ci = lax.axis_index("pair"), lax.axis_index("core")
    capacity = tok_count * expert_ids.shape[1] * 9 // (8 * planes * 8)
    rounds = min(planes, 8)
    group = planes // rounds
    rows = group * 4 * capacity
    held = group * tok_count

    spots = (zi, yi, xi, ci)
    projected, tables = project(
        context,
        w_out,
        expert_ids,
        route_weight,
        spots,
        lambda table: routing_tables(table, spots, capacity, rounds),
    )
    pick_ours, pick_theirs, place_kept, place_sent = tables
    residual = hidden_in.astype(jnp.float32) + projected
    attended = residual.astype(jnp.bfloat16)
    inverse = lax.rsqrt(jnp.mean(residual * residual, axis=1, keepdims=True) + 1e-06)
    normed = (residual * inverse * norm_gain[None, :]).astype(jnp.bfloat16)

    gather = PlaneGather(normed, zi)
    across = [None] * rounds
    ours, leaving, out = [None] * rounds, [None] * rounds, [None] * rounds

    def round_block(step):
        if step == 0 and planes > 1:
            gather.start()
        while len(gather.blocks) < (step + 1) * group:
            ahead = len(gather.blocks) // group - 2
            gather.finish(*([leaving[ahead]] if ahead >= 0 else []))
            if len(gather.blocks) < planes:
                gather.start()
        blocks = gather.blocks[step * group : (step + 1) * group]
        return blocks[0] if group == 1 else jnp.concatenate(blocks)

    def pick_rows(step):
        block = round_block(step)
        if step:
            block = after(block, across[step - 1])
        across[step] = swap(block, "pair")
        tokens = jnp.concatenate(
            [block, swap(block, "core"), across[step], swap(across[step], "core")]
        )
        leaving[step] = dot(pick_theirs[step], tokens).astype(jnp.bfloat16)
        ours[step] = dot(pick_ours[step], tokens).astype(jnp.bfloat16)

    def expert(step, *others):
        theirs = after(swap(leaving[step], "inner"), *others)
        gate_up = dot(jnp.concatenate([ours[step], theirs]), w_gate_up[0])
        act = jax.nn.silu(gate_up[:, :hidden_units]) * gate_up[:, hidden_units:]
        out[step] = dot(act.astype(jnp.bfloat16), w_down[0]).astype(jnp.bfloat16)

    pick_rows(0)
    for step in range(rounds):
        others = []
        if step + 1 < rounds:
            pick_rows(step + 1)
            others.append(leaving[step + 1])
        if step:
            others.append(out[step - 1])
        expert(step, *others)

    pieces = [None] * planes
    came = crossed = sent = None
    for step in range(rounds - 1, -1, -1):
        back = out[step][rows:]
        came = swap(back if came is None else after(back, came), "inner")
        back = came if sent is None else after(came, sent)
        results = jnp.concatenate([out[step][:rows]] * 2 + [back] * 2)
        sent = dot(place_sent[step].reshape(2 * held, -1), results).astype(jnp.bfloat16)
        kept = dot(place_kept[step].reshape(2 * held, -1), results)
        kept = (kept + swap(sent, "core").astype(jnp.float32)).reshape(2, held, width)
        sent = kept[1].astype(jnp.bfloat16)
        crossed = swap(sent if crossed is None else after(sent, crossed), "pair")
        part = (kept[0] + crossed.astype(jnp.float32)).reshape(group, tok_count, width)
        for j in range(group):
            pieces[step * group + j] = part[j]
    total = residual + pieces[0] + scatter_planes(pieces, zi)
    return attended, total.astype(jnp.bfloat16)


def solution(mesh):
    experts, tensors = mesh.shape["expert"], mesh.shape["tensor"]
    split = Mesh(
        mesh.devices.reshape(experts // 2, 2, tensors // 2, 2), ("outer", "inner", "pair", "core")
    )
    expert, tensor = ("outer", "inner"), ("pair", "core")
    every = expert + tensor
    in_specs = (
        P(every, None),
        P(expert, tensor),
        P(tensor, expert),
        P(),
        P(every, None),
        P(every, None),
        P(every, None, None),
        P(every, None, None),
    )
    out_specs = (P(every, None), P(every, None))
    return jax.shard_map(
        on_device, mesh=split, in_specs=in_specs, out_specs=out_specs, check_vma=False
    )
```

time: 847 us -> 507 us (0.60)
  blocking collectives: 233 us -> 0 us
  waiting for transfers between devices: 422 us -> 308 us
  local copies, waits for them, and re-layouts: 100 us -> 6.69 us
  starting transfers between devices: 4.35 us -> 75.6 us
  matrix products: 40.8 us -> 79.7 us
  other arithmetic: 30 us -> 17.9 us
    ppermute x0 -> x67, waiting for transfers between devices: none -> 308 us  [the longest x43 185 us: swap(): return lax.ppermute(array, axis, SWAP)]
    all_to_all x1 -> x0, blocking collectives: 233 us -> none  [on_device(): lax.all_to_all(send_buffer, ('expert', 'tensor'), split_axis=0, concat_ax...]
    all_to_all x1 -> x0, waiting for transfers between devices: 232 us -> none  [on_device(): lax.all_to_all(outputs, ('expert', 'tensor'), split_axis=0, concat_axis=0...]
    all_gather x1 -> x0, waiting for transfers between devices: 130 us -> none  [on_device(): lax.all_gather(w_out, 'expert', axis=1, tiled=True)]
    ppermute x0 -> x67, starting transfers between devices: none -> 75.6 us  [the longest x43 36.5 us: swap(): return lax.ppermute(array, axis, SWAP)]
    reduce_scatter x1 -> x0, waiting for transfers between devices: 59.5 us -> none  [on_device(): lax.psum_scatter(partial_sums, 'tensor', scatter_dimension=0, tiled=True)]
    reshape x4 -> x0, local copies, waits for them, and re-layouts: 52.8 us -> none  [the longest x1 13.3 us: expert_block(): flattened = received.reshape(-1, block_shape[-1])]
    dot_general x3 -> x34, matrix products: 40.8 us -> 79.7 us  [dot(): return jnp.dot(a, b, preferred_element_type=jnp.float32)]
  transfers between devices with their start and end apart: 3 -> 67, of which waited for: 3 -> 33; matrix products, arithmetic and copies ran while one was open for 1% -> 16% of each run, Pallas kernels for 0% -> 0%
where the time goes in v1:
time: 507 us; the launch traced here: 497 us
  waiting for transfers between devices  308 us (61%)
  matrix products  79.7 us (16%)
  starting transfers between devices  75.6 us (15%)
  other arithmetic  17.9 us (4%)
  between operations  9.53 us (2%)
  local copies, waits for them, and re-layouts  6.69 us (1%)
    ppermute x43, waiting for transfers between devices, swap(): return lax.ppermute(array, axis, SWAP)  185 us
    dot_general x34, matrix products, dot(): return jnp.dot(a, b, preferred_element_type=jnp.float32)  79.7 us
    ppermute x9, waiting for transfers between devices, start(): lax.ppermute(self.down, 'outer', [(i, i - 1) for i in range(1, planes - h...  76 us
    ppermute x3, waiting for transfers between devices, scatter_planes(): lax.ppermute(up.astype(jnp.bfloat16), 'outer', [(i, i + 1) for i in range...  41.6 us
    ppermute x43, starting transfers between devices, swap(): return lax.ppermute(array, axis, SWAP)  36.5 us
    ppermute x9, starting transfers between devices, start(): lax.ppermute(self.up, 'outer', [(i, i + 1) for i in range(hop - 1, planes...  18.3 us
    ppermute x9, starting transfers between devices, start(): lax.ppermute(self.down, 'outer', [(i, i - 1) for i in range(1, planes - h...  11.6 us
  transfers between devices with their start and end apart: 67, of which 33 were waited for; matrix products, arithmetic and copies ran while one was open for 16% of the time, Pallas kernels for 0%

profile of v1, /device:TPU:0, one launch (start us, length us, event | category | flops | bytes accessed | tf_op | source)
XLA Modules:
  0.0 497.3 jit_solution(11887865265041639826)
XLA Ops:
  0.6 3.0 collective-permute-start
  4.9 4.6 collective-permute-start.4
  13.8 13.2 %collective-permute-done = bf16[512,1024]{1,0:T(8,128)(2,1)S(1)} collective-permute-done((bf16[512,1024]{1,0:T(8,128)(2,1)}, bf16[512,1024]{1,0:T(8,128)(2,1)S(1)}, u32[]{:S(2)}, u32[]{:S(2)}) %collective-permute-start) | collective-permute-done | bytes 1048608 | tf_op jit(solution)/shard_map/ppermute | solution.py:10
  31.2 3.7 collective-permute-start.21
  54.9 5.2 %collective-permute-done.2 = bf16[2,128,512]{2,1,0:T(8,128)(2,1)S(1)} collective-permute-done((bf16[2,128,512]{2,1,0:T(8,128)(2,1)S(1)}, bf16[2,128,512]{2,1,0:T(8,128)(2,1)S(1)}, u32[]{:S(2)}, u32[]{:S(2)}) %collective-permute-start.2) | collective-permute-done | bytes 262176 | tf_op jit(solution)/shard_map/ppermute | solution.py:10
  61.7 12.0 %collective-permute-done.10 = bf16[1024,512]{1,0:T(8,128)(2,1)S(1)} collective-permute-done((bf16[1024,512]{1,0:T(8,128)(2,1)S(1)}, bf16[1024,512]{1,0:T(8,128)(2,1)S(1)}, u32[]{:S(2)}, u32[]{:S(2)}) %collective-permute-start.10) | collective-permute-done | bytes 1048608 | tf_op jit(solution)/shard_map/ppermute | solution.py:41
  80.4 3.4 collective-permute-done.8
  86.0 16.0 %collective-permute-done.15 = bf16[1024,512]{1,0:T(8,128)(2,1)S(1)} collective-permute-done((bf16[1024,512]{1,0:T(8,128)(2,1)S(1)}, bf16[1024,512]{1,0:T(8,128)(2,1)S(1)}, u32[]{:S(2)}, u32[]{:S(2)}) %collective-permute-start.15) | collective-permute-done | bytes 1048608 | tf_op jit(solution)/shard_map/ppermute | solution.py:41
  113.0 6.3 %collective-permute-done.17 = bf16[2,128,512]{2,1,0:T(8,128)(2,1)S(1)} collective-permute-done((bf16[2,128,512]{2,1,0:T(8,128)(2,1)S(1)}, bf16[2,128,512]{2,1,0:T(8,128)(2,1)S(1)}, u32[]{:S(2)}, u32[]{:S(2)}) %collective-permute-start.17) | collective-permute-done | bytes 262176 | tf_op jit(solution)/shard_map/ppermute | solution.py:10
  119.9 4.1 collective-permute-done.12
  124.8 4.4 collective-permute-done.13
  134.0 5.7 %collective-permute-start.31 = (bf16[128,4096]{1,0:T(8,128)(2,1)}, bf16[128,4096]{1,0:T(8,128)(2,1)}, u32[]{:S(2)}, u32[]{:S(2)}) collective-permute-start(bf16[128,4096]{1,0:T(8,128)(2,1)} %multiply_convert_fusion), channel_id=1, source_target_pairs={{0,8},{8,16},{16,24},{1,9},{9,17},{17,25},{2,10},{10,18},{18,26},{... | collective-permute-start | bytes 3145736 | tf_op jit(solution)/shard_map/ppermute | solution.py:40
  144.0 2.4 pad_maximum_fusion.5
  146.8 11.3 %collective-permute-done.32 = bf16[128,4096]{1,0:T(8,128)(2,1)} collective-permute-done((bf16[128,4096]{1,0:T(8,128)(2,1)}, bf16[128,4096]{1,0:T(8,128)(2,1)}, u32[]{:S(2)}, u32[]{:S(2)}) %collective-permute-start.32) | collective-permute-done | bytes 1048608 | tf_op jit(solution)/shard_map/ppermute | solution.py:41
  167.1 2.6 convolution_convert_fusion.10
  170.3 13.8 %collective-permute-done.38 = bf16[128,4096]{1,0:T(8,128)(2,1)S(1)} collective-permute-done((bf16[128,4096]{1,0:T(8,128)(2,1)}, bf16[128,4096]{1,0:T(8,128)(2,1)S(1)}, u32[]{:S(2)}, u32[]{:S(2)}) %collective-permute-start.38) | collective-permute-done | bytes 1048608 | tf_op jit(solution)/shard_map/ppermute | solution.py:41
  186.1 4.3 collective-permute-done.34
  190.5 2.7 convolution_convert_fusion.11
  194.2 22.6 %collective-permute-done.44 = bf16[128,4096]{1,0:T(8,128)(2,1)S(1)} collective-permute-done((bf16[128,4096]{1,0:T(8,128)(2,1)S(1)}, bf16[128,4096]{1,0:T(8,128)(2,1)S(1)}, u32[]{:S(2)}, u32[]{:S(2)}) %collective-permute-start.44) | collective-permute-done | bytes 1048608 | tf_op jit(solution)/shard_map/ppermute | solution.py:41
  220.8 7.6 %fusion.6 = f32[288,1536]{1,0:T(8,128)S(1)} fusion(bf16[1,4096,1536]{2,1,0:T(8,128)(2,1)} %param.15, bf16[144,4096]{1,0:T(8,128)(2,1)S(1)} %collective-permute-done.30, bf16[144,4096]{1,0:T(8,128)(2,1)S(1)} %convolution_convert_fusion.11), kind=kOutput, calls=%fused_computation.6 | convolution fusion | flops 3628597248 | bytes 16711680 | tf_op jit(solution)/shard_map/dot_general | solution.py:14
  230.5 10.9 %collective-permute-done.40 = bf16[128,4096]{1,0:T(8,128)(2,1)S(1)} collective-permute-done((bf16[128,4096]{1,0:T(8,128)(2,1)S(1)}, bf16[128,4096]{1,0:T(8,128)(2,1)S(1)}, u32[]{:S(2)}, u32[]{:S(2)}) %collective-permute-start.40) | collective-permute-done | bytes 1048608 | tf_op jit(solution)/shard_map/ppermute | solution.py:10
  243.7 3.3 collective-permute-done.41
  249.2 15.6 %collective-permute-done.46 = bf16[128,4096]{1,0:T(8,128)(2,1)S(1)} collective-permute-done((bf16[128,4096]{1,0:T(8,128)(2,1)S(1)}, bf16[128,4096]{1,0:T(8,128)(2,1)S(1)}, u32[]{:S(2)}, u32[]{:S(2)}) %collective-permute-start.46) | collective-permute-done | bytes 1048608 | tf_op jit(solution)/shard_map/ppermute | solution.py:10
  264.8 7.2 %fusion.4 = f32[288,1536]{1,0:T(8,128)S(1)} fusion(bf16[1,4096,1536]{2,1,0:T(8,128)(2,1)} %param.15, bf16[144,4096]{1,0:T(8,128)(2,1)} %collective-permute-done.36, bf16[144,4096]{1,0:T(8,128)(2,1)S(1)} %convolution_convert_fusion.8), kind=kOutput, calls=%fused_computation.4 | convolution fusion | flops 3628597248 | bytes 16711680 | tf_op jit(solution)/shard_map/dot_general | solution.py:14
  278.1 7.1 %fusion.2 = f32[288,1536]{1,0:T(8,128)S(1)} fusion(bf16[1,4096,1536]{2,1,0:T(8,128)(2,1)} %param.15, bf16[144,4096]{1,0:T(8,128)(2,1)S(1)} %collective-permute-done.42, bf16[144,4096]{1,0:T(8,128)(2,1)S(1)} %convolution_convert_fusion.6), kind=kOutput, calls=%fused_computation.2 | convolution fusion | flops 3628597248 | bytes 16711680 | tf_op jit(solution)/shard_map/dot_general | solution.py:14
  287.2 17.2 %collective-permute-done.48 = bf16[144,4096]{1,0:T(8,128)(2,1)S(1)} collective-permute-done((bf16[144,4096]{1,0:T(8,128)(2,1)S(1)}, bf16[144,4096]{1,0:T(8,128)(2,1)S(1)}, u32[]{:S(2)}, u32[]{:S(2)}) %collective-permute-start.48) | collective-permute-done | bytes 1179680 | tf_op jit(solution)/shard_map/ppermute | solution.py:10
  304.4 6.9 %fusion = f32[288,1536]{1,0:T(8,128)S(1)} fusion(bf16[1,4096,1536]{2,1,0:T(8,128)(2,1)} %param.15, bf16[144,4096]{1,0:T(8,128)(2,1)S(1)} %collective-permute-done.48, bf16[144,4096]{1,0:T(8,128)(2,1)S(1)} %convolution_convert_fusion.4), kind=kOutput, calls=%fused_computation | convolution fusion | flops 3628597248 | bytes 16711680 | tf_op jit(solution)/shard_map/dot_general | solution.py:14
  314.9 26.3 %collective-permute-done.49 = bf16[144,4096]{1,0:T(8,128)(2,1)S(1)} collective-permute-done((bf16[144,4096]{1,0:T(8,128)(2,1)S(1)}, bf16[144,4096]{1,0:T(8,128)(2,1)S(1)}, u32[]{:S(2)}, u32[]{:S(2)}) %collective-permute-start.49) | collective-permute-done | bytes 1179680 | tf_op jit(solution)/shard_map/ppermute | solution.py:10
  341.2 2.5 convolution_convert_fusion.3
  345.5 2.5 collective-permute-done.53
  348.0 2.3 convolution_add_fusion
  350.5 22.1 %collective-permute-done.50 = bf16[144,4096]{1,0:T(8,128)(2,1)S(1)} collective-permute-done((bf16[144,4096]{1,0:T(8,128)(2,1)S(1)}, bf16[144,4096]{1,0:T(8,128)(2,1)S(1)}, u32[]{:S(2)}, u32[]{:S(2)}) %collective-permute-start.50) | collective-permute-done | bytes 1179680 | tf_op jit(solution)/shard_map/ppermute | solution.py:10
  372.6 2.5 convolution_convert_fusion.2
  378.3 22.5 %collective-permute-done.57 = bf16[128,4096]{1,0:T(8,128)(2,1)S(1)} collective-permute-done((bf16[128,4096]{1,0:T(8,128)(2,1)S(1)}, bf16[128,4096]{1,0:T(8,128)(2,1)S(1)}, u32[]{:S(2)}, u32[]{:S(2)}) %collective-permute-start.57) | collective-permute-done | bytes 1048608 | tf_op jit(solution)/shard_map/ppermute | solution.py:10
  401.7 2.7 collective-permute-start.61
  404.5 2.4 convert_add_fusion.2
  408.5 2.5 convolution_convert_fusion.1
  412.7 13.9 %collective-permute-done.61 = bf16[128,4096]{1,0:T(8,128)(2,1)S(1)} collective-permute-done((bf16[128,4096]{1,0:T(8,128)(2,1)S(1)}, bf16[128,4096]{1,0:T(8,128)(2,1)S(1)}, u32[]{:S(2)}, u32[]{:S(2)}) %collective-permute-start.61) | collective-permute-done | bytes 1048608 | tf_op jit(solution)/shard_map/ppermute | solution.py:173
  426.6 4.9 collective-permute-done.58
  434.8 2.6 convert_add_fusion.1
  437.5 2.4 collective-permute-done.52
  440.4 2.5 convolution_convert_fusion
  443.0 12.3 %collective-permute-done.62 = bf16[128,4096]{1,0:T(8,128)(2,1)S(1)} collective-permute-done((bf16[128,4096]{1,0:T(8,128)(2,1)S(1)}, bf16[128,4096]{1,0:T(8,128)(2,1)S(1)}, u32[]{:S(2)}, u32[]{:S(2)}) %collective-permute-start.62) | collective-permute-done | bytes 1048608 | tf_op jit(solution)/shard_map/ppermute | solution.py:173
  455.3 9.3 %collective-permute-done.59 = bf16[128,4096]{1,0:T(8,128)(2,1)S(1)} collective-permute-done((bf16[128,4096]{1,0:T(8,128)(2,1)S(1)}, bf16[128,4096]{1,0:T(8,128)(2,1)S(1)}, u32[]{:S(2)}, u32[]{:S(2)}) %collective-permute-start.59) | collective-permute-done | bytes 1048608 | tf_op jit(solution)/shard_map/ppermute | solution.py:10
  469.1 2.4 convert_add_fusion
  473.2 15.4 %collective-permute-done.63 = bf16[128,4096]{1,0:T(8,128)(2,1)S(1)} collective-permute-done((bf16[128,4096]{1,0:T(8,128)(2,1)S(1)}, bf16[128,4096]{1,0:T(8,128)(2,1)S(1)}, u32[]{:S(2)}, u32[]{:S(2)}) %collective-permute-start.63) | collective-permute-done | bytes 1048608 | tf_op jit(solution)/shard_map/ppermute | solution.py:173
  488.6 4.2 collective-permute-done.66
  494.8 2.3 fusion.44
  (237 shorter events, 110.1 us)
Async XLA Ops:
  0.6 26.4 %collective-permute-start = (bf16[512,1024]{1,0:T(8,128)(2,1)}, bf16[512,1024]{1,0:T(8,128)(2,1)S(1)}, u32[]{:S(2)}, u32[]{:S(2)}) collective-permute-start(bf16[512,1024]{1,0:T(8,128)(2,1)} %param.10), channel_id=1, source_target_pairs={{0,4},{4,0},{1,5},{5,1},{2,6},{6,2},{3,7},{7,3},{8,12},{12,8},{9,1... | collective-permute-start | bytes 3145736 | tf_op jit(solution)/shard_map/ppermute | solution.py:10
  3.7 32.6 %collective-permute-start.5 = (bf16[1024,512]{1,0:T(8,128)(2,1)}, bf16[1024,512]{1,0:T(8,128)(2,1)S(1)}, u32[]{:S(2)}, u32[]{:S(2)}) collective-permute-start(bf16[1024,512]{1,0:T(8,128)(2,1)} %param.11), channel_id=1, source_target_pairs={{8,0},{16,8},{24,16},{9,1},{17,9},{25,17},{10,2},{18,10},{26,18},{... | collective-permute-start | bytes 3145736 | tf_op jit(solution)/shard_map/ppermute | solution.py:41
  4.9 31.3 %collective-permute-start.4 = (bf16[1024,512]{1,0:T(8,128)(2,1)}, bf16[1024,512]{1,0:T(8,128)(2,1)S(1)}, u32[]{:S(2)}, u32[]{:S(2)}) collective-permute-start(bf16[1024,512]{1,0:T(8,128)(2,1)} %param.11), channel_id=1, source_target_pairs={{0,8},{8,16},{16,24},{1,9},{9,17},{17,25},{2,10},{10,18},{18,26},{... | collective-permute-start | bytes 3145736 | tf_op jit(solution)/shard_map/ppermute | solution.py:40
  12.3 19.0 %collective-permute-start.20 = (f32[2,128,16]{1,2,0:T(8,128)S(1)}, f32[2,128,16]{1,2,0:T(8,128)S(1)}, u32[]{:S(2)}, u32[]{:S(2)}) collective-permute-start(f32[2,128,16]{1,2,0:T(8,128)S(1)} %get-tuple-element.130), channel_id=1, source_target_pairs={{0,2},{2,0},{1,3},{3,1},{4,6},{6,4},{5,7},{7,5},{8,10},{10,8},{9,1... | collective-permute-start | bytes 49160 | tf_op jit(solution)/shard_map/ppermute | solution.py:10
  31.2 17.5 %collective-permute-start.1 = (bf16[512,512]{1,0:T(8,128)(2,1)}, bf16[512,512]{1,0:T(8,128)(2,1)}, u32[]{:S(2)}, u32[]{:S(2)}) collective-permute-start(bf16[512,512]{1,0:T(8,128)(2,1)} %convolution_convert_fusion.15), channel_id=1, source_target_pairs={{0,1},{1,0},{2,3},{3,2},{4,5},{5,4},{6,7},{7,6},{8,9},{9,8},{10,11... | collective-permute-start | bytes 1572872 | tf_op jit(solution)/shard_map/ppermute | solution.py:10
  45.4 28.3 %collective-permute-start.10 = (bf16[1024,512]{1,0:T(8,128)(2,1)S(1)}, bf16[1024,512]{1,0:T(8,128)(2,1)S(1)}, u32[]{:S(2)}, u32[]{:S(2)}) collective-permute-start(bf16[1024,512]{1,0:T(8,128)(2,1)S(1)} %collective-permute-done.5), channel_id=1, source_target_pairs={{8,0},{16,8},{9,1},{17,9},{10,2},{18,10},{11,3},{19,11},{12,4},{20... | collective-permute-start | bytes 3145736 | tf_op jit(solution)/shard_map/ppermute | solution.py:41
  46.7 28.6 %collective-permute-start.9 = (bf16[1024,512]{1,0:T(8,128)(2,1)S(1)}, bf16[1024,512]{1,0:T(8,128)(2,1)S(1)}, u32[]{:S(2)}, u32[]{:S(2)}) collective-permute-start(bf16[1024,512]{1,0:T(8,128)(2,1)S(1)} %collective-permute-done.4), channel_id=1, source_target_pairs={{8,16},{16,24},{9,17},{17,25},{10,18},{18,26},{11,19},{19,27},{12,... | collective-permute-start | bytes 3145736 | tf_op jit(solution)/shard_map/ppermute | solution.py:40
  47.4 36.4 %collective-permute-start.24 = (f32[2,2,128,16]{2,3,1,0:T(8,128)S(1)}, f32[2,2,128,16]{2,3,1,0:T(8,128)S(1)}, u32[]{:S(2)}, u32[]{:S(2)}) collective-permute-start(f32[2,2,128,16]{2,3,1,0:T(8,128)S(1)} %collective-permute-done.22), channel_id=1, source_target_pairs={{8,0},{16,8},{9,1},{17,9},{10,2},{18,10},{11,3},{19,11},{12,4},{20... | collective-permute-start | bytes 98312 | tf_op jit(solution)/shard_map/ppermute | solution.py:41
  48.8 35.1 %collective-permute-start.23 = (f32[2,2,128,16]{2,3,1,0:T(8,128)S(1)}, f32[2,2,128,16]{2,3,1,0:T(8,128)S(1)}, u32[]{:S(2)}, u32[]{:S(2)}) collective-permute-start(f32[2,2,128,16]{2,3,1,0:T(8,128)S(1)} %collective-permute-done.21), channel_id=1, source_target_pairs={{8,16},{16,24},{9,17},{17,25},{10,18},{18,26},{11,19},{19,27},{12,... | collective-permute-start | bytes 98312 | tf_op jit(solution)/shard_map/ppermute | solution.py:40
  60.1 16.4 %collective-permute-start.7 = (bf16[2,128,512]{2,1,0:T(8,128)(2,1)S(1)}, bf16[2,128,512]{2,1,0:T(8,128)(2,1)S(1)}, u32[]{:S(2)}, u32[]{:S(2)}) collective-permute-start(bf16[2,128,512]{2,1,0:T(8,128)(2,1)S(1)} %fusion.70), channel_id=1, source_target_pairs={{0,2},{2,0},{1,3},{3,1},{4,6},{6,4},{5,7},{7,5},{8,10},{10,8},{9,1... | collective-permute-start | bytes 786440 | tf_op jit(solution)/shard_map/ppermute | solution.py:10
  75.3 26.7 %collective-permute-start.15 = (bf16[1024,512]{1,0:T(8,128)(2,1)S(1)}, bf16[1024,512]{1,0:T(8,128)(2,1)S(1)}, u32[]{:S(2)}, u32[]{:S(2)}) collective-permute-start(bf16[1024,512]{1,0:T(8,128)(2,1)S(1)} %collective-permute-done.10), channel_id=1, source_target_pairs={{8,0},{9,1},{10,2},{11,3},{12,4},{13,5},{14,6},{15,7}} | collective-permute-start | bytes 3145736 | tf_op jit(solution)/shard_map/ppermute | solution.py:41
  76.6 25.4 %collective-permute-start.14 = (bf16[1024,512]{1,0:T(8,128)(2,1)S(1)}, bf16[1024,512]{1,0:T(8,128)(2,1)S(1)}, u32[]{:S(2)}, u32[]{:S(2)}) collective-permute-start(bf16[1024,512]{1,0:T(8,128)(2,1)S(1)} %collective-permute-done.9), channel_id=1, source_target_pairs={{16,24},{17,25},{18,26},{19,27},{20,28},{21,29},{22,30},{23,31}} | collective-permute-start | bytes 3145736 | tf_op jit(solution)/shard_map/ppermute | solution.py:40
  83.9 18.4 %collective-permute-start.26 = (f32[2,2,128,16]{2,3,1,0:T(8,128)S(1)}, f32[2,2,128,16]{2,3,1,0:T(8,128)S(1)}, u32[]{:S(2)}, u32[]{:S(2)}) collective-permute-start(f32[2,2,128,16]{2,3,1,0:T(8,128)S(1)} %collective-permute-done.24), channel_id=1, source_target_pairs={{8,0},{9,1},{10,2},{11,3},{12,4},{13,5},{14,6},{15,7}} | collective-permute-start | bytes 98312 | tf_op jit(solution)/shard_map/ppermute | solution.py:41
  85.2 17.1 %collective-permute-start.25 = (f32[2,2,128,16]{2,3,1,0:T(8,128)S(1)}, f32[2,2,128,16]{2,3,1,0:T(8,128)S(1)}, u32[]{:S(2)}, u32[]{:S(2)}) collective-permute-start(f32[2,2,128,16]{2,3,1,0:T(8,128)S(1)} %collective-permute-done.23), channel_id=1, source_target_pairs={{16,24},{17,25},{18,26},{19,27},{20,28},{21,29},{22,30},{23,31}} | collective-permute-start | bytes 98312 | tf_op jit(solution)/shard_map/ppermute | solution.py:40
  132.7 25.4 %collective-permute-start.32 = (bf16[128,4096]{1,0:T(8,128)(2,1)}, bf16[128,4096]{1,0:T(8,128)(2,1)}, u32[]{:S(2)}, u32[]{:S(2)}) collective-permute-start(bf16[128,4096]{1,0:T(8,128)(2,1)} %multiply_convert_fusion), channel_id=1, source_target_pairs={{8,0},{16,8},{24,16},{9,1},{17,9},{25,17},{10,2},{18,10},{26,18},{... | collective-permute-start | bytes 3145736 | tf_op jit(solution)/shard_map/ppermute | solution.py:41
  134.0 25.3 %collective-permute-start.31 = (bf16[128,4096]{1,0:T(8,128)(2,1)}, bf16[128,4096]{1,0:T(8,128)(2,1)}, u32[]{:S(2)}, u32[]{:S(2)}) collective-permute-start(bf16[128,4096]{1,0:T(8,128)(2,1)} %multiply_convert_fusion), channel_id=1, source_target_pairs={{0,8},{8,16},{16,24},{1,9},{9,17},{17,25},{2,10},{10,18},{18,26},{... | collective-permute-start | bytes 3145736 | tf_op jit(solution)/shard_map/ppermute | solution.py:40
  139.7 23.0 %collective-permute-start.28 = (bf16[128,4096]{1,0:T(8,128)(2,1)}, bf16[128,4096]{1,0:T(8,128)(2,1)}, u32[]{:S(2)}, u32[]{:S(2)}) collective-permute-start(bf16[128,4096]{1,0:T(8,128)(2,1)} %multiply_convert_fusion), channel_id=1, source_target_pairs={{0,2},{2,0},{1,3},{3,1},{4,6},{6,4},{5,7},{7,5},{8,10},{10,8},{9,1... | collective-permute-start | bytes 3145736 | tf_op jit(solution)/shard_map/ppermute | solution.py:10
  146.5 19.9 %collective-permute-start.27 = (bf16[128,4096]{1,0:T(8,128)(2,1)}, bf16[128,4096]{1,0:T(8,128)(2,1)}, u32[]{:S(2)}, u32[]{:S(2)}) collective-permute-start(bf16[128,4096]{1,0:T(8,128)(2,1)} %multiply_convert_fusion), channel_id=1, source_target_pairs={{0,1},{1,0},{2,3},{3,2},{4,5},{5,4},{6,7},{7,6},{8,9},{9,8},{10,11... | collective-permute-start | bytes 3145736 | tf_op jit(solution)/shard_map/ppermute | solution.py:10
  159.3 24.9 %collective-permute-start.38 = (bf16[128,4096]{1,0:T(8,128)(2,1)}, bf16[128,4096]{1,0:T(8,128)(2,1)S(1)}, u32[]{:S(2)}, u32[]{:S(2)}) collective-permute-start(bf16[128,4096]{1,0:T(8,128)(2,1)} %collective-permute-done.32), channel_id=1, source_target_pairs={{8,0},{16,8},{9,1},{17,9},{10,2},{18,10},{11,3},{19,11},{12,4},{20... | collective-permute-start | bytes 3145736 | tf_op jit(solution)/shard_map/ppermute | solution.py:41
  164.1 20.0 %collective-permute-start.37 = (bf16[128,4096]{1,0:T(8,128)(2,1)}, bf16[128,4096]{1,0:T(8,128)(2,1)S(1)}, u32[]{:S(2)}, u32[]{:S(2)}) collective-permute-start(bf16[128,4096]{1,0:T(8,128)(2,1)} %collective-permute-done.31), channel_id=1, source_target_pairs={{8,16},{16,24},{9,17},{17,25},{10,18},{18,26},{11,19},{19,27},{12,... | collective-permute-start | bytes 3145736 | tf_op jit(solution)/shard_map/ppermute | solution.py:40
  164.8 25.6 %collective-permute-start.34 = (bf16[128,4096]{1,0:T(8,128)(2,1)S(1)}, bf16[128,4096]{1,0:T(8,128)(2,1)S(1)}, u32[]{:S(2)}, u32[]{:S(2)}) collective-permute-start(bf16[128,4096]{1,0:T(8,128)(2,1)S(1)} %broadcast_select_fusion), channel_id=1, source_target_pairs={{0,2},{2,0},{1,3},{3,1},{4,6},{6,4},{5,7},{7,5},{8,10},{10,8},{9,1... | collective-permute-start | bytes 3145736 | tf_op jit(solution)/shard_map/ppermute | solution.py:10
  166.4 24.1 %collective-permute-start.33 = (bf16[128,4096]{1,0:T(8,128)(2,1)S(1)}, bf16[128,4096]{1,0:T(8,128)(2,1)S(1)}, u32[]{:S(2)}, u32[]{:S(2)}) collective-permute-start(bf16[128,4096]{1,0:T(8,128)(2,1)S(1)} %broadcast_select_fusion), channel_id=1, source_target_pairs={{0,1},{1,0},{2,3},{3,2},{4,5},{5,4},{6,7},{7,6},{8,9},{9,8},{10,11... | collective-permute-start | bytes 3145736 | tf_op jit(solution)/shard_map/ppermute | solution.py:10
  169.7 51.1 %collective-permute-start.30 = (bf16[144,4096]{1,0:T(8,128)(2,1)S(1)}, bf16[144,4096]{1,0:T(8,128)(2,1)S(1)}, u32[]{:S(2)}, u32[]{:S(2)}) collective-permute-start(bf16[144,4096]{1,0:T(8,128)(2,1)S(1)} %convolution_convert_fusion.10), channel_id=1, source_target_pairs={{0,4},{4,0},{1,5},{5,1},{2,6},{6,2},{3,7},{7,3},{8,12},{12,8},{9,1... | collective-permute-start | bytes 3538952 | tf_op jit(solution)/shard_map/ppermute | solution.py:10
  184.1 32.6 %collective-permute-start.44 = (bf16[128,4096]{1,0:T(8,128)(2,1)S(1)}, bf16[128,4096]{1,0:T(8,128)(2,1)S(1)}, u32[]{:S(2)}, u32[]{:S(2)}) collective-permute-start(bf16[128,4096]{1,0:T(8,128)(2,1)S(1)} %collective-permute-done.38), channel_id=1, source_target_pairs={{8,0},{9,1},{10,2},{11,3},{12,4},{13,5},{14,6},{15,7}} | collective-permute-start | bytes 3145736 | tf_op jit(solution)/shard_map/ppermute | solution.py:41
  185.4 31.3 %collective-permute-start.43 = (bf16[128,4096]{1,0:T(8,128)(2,1)S(1)}, bf16[128,4096]{1,0:T(8,128)(2,1)S(1)}, u32[]{:S(2)}, u32[]{:S(2)}) collective-permute-start(bf16[128,4096]{1,0:T(8,128)(2,1)S(1)} %collective-permute-done.37), channel_id=1, source_target_pairs={{16,24},{17,25},{18,26},{19,27},{20,28},{21,29},{22,30},{23,31}} | collective-permute-start | bytes 3145736 | tf_op jit(solution)/shard_map/ppermute | solution.py:40
  217.2 24.3 %collective-permute-start.40 = (bf16[128,4096]{1,0:T(8,128)(2,1)S(1)}, bf16[128,4096]{1,0:T(8,128)(2,1)S(1)}, u32[]{:S(2)}, u32[]{:S(2)}) collective-permute-start(bf16[128,4096]{1,0:T(8,128)(2,1)S(1)} %get-tuple-element.61), channel_id=1, source_target_pairs={{0,2},{2,0},{1,3},{3,1},{4,6},{6,4},{5,7},{7,5},{8,10},{10,8},{9,1... | collective-permute-start | bytes 3145736 | tf_op jit(solution)/shard_map/ppermute | solution.py:10
  218.7 24.8 %collective-permute-start.39 = (bf16[128,4096]{1,0:T(8,128)(2,1)S(1)}, bf16[128,4096]{1,0:T(8,128)(2,1)S(1)}, u32[]{:S(2)}, u32[]{:S(2)}) collective-permute-start(bf16[128,4096]{1,0:T(8,128)(2,1)S(1)} %get-tuple-element.61), channel_id=1, source_target_pairs={{0,1},{1,0},{2,3},{3,2},{4,5},{5,4},{6,7},{7,6},{8,9},{9,8},{10,11... | collective-permute-start | bytes 3145736 | tf_op jit(solution)/shard_map/ppermute | solution.py:10
  218.7 30.5 %collective-permute-start.36 = (bf16[144,4096]{1,0:T(8,128)(2,1)S(1)}, bf16[144,4096]{1,0:T(8,128)(2,1)}, u32[]{:S(2)}, u32[]{:S(2)}) collective-permute-start(bf16[144,4096]{1,0:T(8,128)(2,1)S(1)} %convolution_convert_fusion.9), channel_id=1, source_target_pairs={{0,4},{4,0},{1,5},{5,1},{2,6},{6,2},{3,7},{7,3},{8,12},{12,8},{9,1... | collective-permute-start | bytes 3538952 | tf_op jit(solution)/shard_map/ppermute | solution.py:10
  241.4 23.4 %collective-permute-start.46 = (bf16[128,4096]{1,0:T(8,128)(2,1)S(1)}, bf16[128,4096]{1,0:T(8,128)(2,1)S(1)}, u32[]{:S(2)}, u32[]{:S(2)}) collective-permute-start(bf16[128,4096]{1,0:T(8,128)(2,1)S(1)} %get-tuple-element.65), channel_id=1, source_target_pairs={{0,2},{2,0},{1,3},{3,1},{4,6},{6,4},{5,7},{7,5},{8,10},{10,8},{9,1... | collective-permute-start | bytes 3145736 | tf_op jit(solution)/shard_map/ppermute | solution.py:10
  242.9 29.1 %collective-permute-start.45 = (bf16[128,4096]{1,0:T(8,128)(2,1)S(1)}, bf16[128,4096]{1,0:T(8,128)(2,1)S(1)}, u32[]{:S(2)}, u32[]{:S(2)}) collective-permute-start(bf16[128,4096]{1,0:T(8,128)(2,1)S(1)} %get-tuple-element.65), channel_id=1, source_target_pairs={{0,1},{1,0},{2,3},{3,2},{4,5},{5,4},{6,7},{7,6},{8,9},{9,8},{10,11... | collective-permute-start | bytes 3145736 | tf_op jit(solution)/shard_map/ppermute | solution.py:10
  248.0 30.1 %collective-permute-start.42 = (bf16[144,4096]{1,0:T(8,128)(2,1)S(1)}, bf16[144,4096]{1,0:T(8,128)(2,1)S(1)}, u32[]{:S(2)}, u32[]{:S(2)}) collective-permute-start(bf16[144,4096]{1,0:T(8,128)(2,1)S(1)} %convolution_convert_fusion.7), channel_id=1, source_target_pairs={{0,4},{4,0},{1,5},{5,1},{2,6},{6,2},{3,7},{7,3},{8,12},{12,8},{9,1... | collective-permute-start | bytes 3538952 | tf_op jit(solution)/shard_map/ppermute | solution.py:10
  276.0 28.4 %collective-permute-start.48 = (bf16[144,4096]{1,0:T(8,128)(2,1)S(1)}, bf16[144,4096]{1,0:T(8,128)(2,1)S(1)}, u32[]{:S(2)}, u32[]{:S(2)}) collective-permute-start(bf16[144,4096]{1,0:T(8,128)(2,1)S(1)} %convolution_convert_fusion.5), channel_id=1, source_target_pairs={{0,4},{4,0},{1,5},{5,1},{2,6},{6,2},{3,7},{7,3},{8,12},{12,8},{9,1... | collective-permute-start | bytes 3538952 | tf_op jit(solution)/shard_map/ppermute | solution.py:10
  313.6 27.7 %collective-permute-start.49 = (bf16[144,4096]{1,0:T(8,128)(2,1)S(1)}, bf16[144,4096]{1,0:T(8,128)(2,1)S(1)}, u32[]{:S(2)}, u32[]{:S(2)}) collective-permute-start(bf16[144,4096]{1,0:T(8,128)(2,1)S(1)} %get-tuple-element.97), channel_id=1, source_target_pairs={{0,4},{4,0},{1,5},{5,1},{2,6},{6,2},{3,7},{7,3},{8,12},{12,8},{9,1... | collective-permute-start | bytes 3538952 | tf_op jit(solution)/shard_map/ppermute | solution.py:10
  344.1 28.4 %collective-permute-start.50 = (bf16[144,4096]{1,0:T(8,128)(2,1)S(1)}, bf16[144,4096]{1,0:T(8,128)(2,1)S(1)}, u32[]{:S(2)}, u32[]{:S(2)}) collective-permute-start(bf16[144,4096]{1,0:T(8,128)(2,1)S(1)} %get-tuple-element.68), channel_id=1, source_target_pairs={{0,4},{4,0},{1,5},{5,1},{2,6},{6,2},{3,7},{7,3},{8,12},{12,8},{9,1... | collective-permute-start | bytes 3538952 | tf_op jit(solution)/shard_map/ppermute | solution.py:10
  375.1 29.4 %collective-permute-start.54 = (bf16[256,4096]{1,0:T(8,128)(2,1)S(1)}, bf16[256,4096]{1,0:T(8,128)(2,1)S(1)}, u32[]{:S(2)}, u32[]{:S(2)}) collective-permute-start(bf16[256,4096]{1,0:T(8,128)(2,1)S(1)} %convolution_convert_fusion.2), channel_id=1, source_target_pairs={{0,1},{1,0},{2,3},{3,2},{4,5},{5,4},{6,7},{7,6},{8,9},{9,8},{10,11... | collective-permute-start | bytes 6291464 | tf_op jit(solution)/shard_map/ppermute | solution.py:10
  375.2 25.6 %collective-permute-start.57 = (bf16[128,4096]{1,0:T(8,128)(2,1)S(1)}, bf16[128,4096]{1,0:T(8,128)(2,1)S(1)}, u32[]{:S(2)}, u32[]{:S(2)}) collective-permute-start(bf16[128,4096]{1,0:T(8,128)(2,1)S(1)} %slice.415), channel_id=1, source_target_pairs={{0,2},{2,0},{1,3},{3,1},{4,6},{6,4},{5,7},{7,5},{8,10},{10,8},{9,1... | collective-permute-start | bytes 3145736 | tf_op jit(solution)/shard_map/ppermute | solution.py:10
  377.0 31.6 %collective-permute-start.51 = (bf16[144,4096]{1,0:T(8,128)(2,1)S(1)}, bf16[144,4096]{1,0:T(8,128)(2,1)S(1)}, u32[]{:S(2)}, u32[]{:S(2)}) collective-permute-start(bf16[144,4096]{1,0:T(8,128)(2,1)S(1)} %get-tuple-element.69), channel_id=1, source_target_pairs={{0,4},{4,0},{1,5},{5,1},{2,6},{6,2},{3,7},{7,3},{8,12},{12,8},{9,1... | collective-permute-start | bytes 3538952 | tf_op jit(solution)/shard_map/ppermute | solution.py:10
  401.7 24.9 %collective-permute-start.61 = (bf16[128,4096]{1,0:T(8,128)(2,1)S(1)}, bf16[128,4096]{1,0:T(8,128)(2,1)S(1)}, u32[]{:S(2)}, u32[]{:S(2)}) collective-permute-start(bf16[128,4096]{1,0:T(8,128)(2,1)S(1)} %fusion.60), channel_id=1, source_target_pairs={{0,8},{1,9},{2,10},{3,11},{4,12},{5,13},{6,14},{7,15}} | collective-permute-start | bytes 3145736 | tf_op jit(solution)/shard_map/ppermute | solution.py:173
  407.0 24.5 %collective-permute-start.58 = (bf16[128,4096]{1,0:T(8,128)(2,1)S(1)}, bf16[128,4096]{1,0:T(8,128)(2,1)S(1)}, u32[]{:S(2)}, u32[]{:S(2)}) collective-permute-start(bf16[128,4096]{1,0:T(8,128)(2,1)S(1)} %slice.414), channel_id=1, source_target_pairs={{0,2},{2,0},{1,3},{3,1},{4,6},{6,4},{5,7},{7,5},{8,10},{10,8},{9,1... | collective-permute-start | bytes 3145736 | tf_op jit(solution)/shard_map/ppermute | solution.py:10
  411.1 23.7 %collective-permute-start.55 = (bf16[256,4096]{1,0:T(8,128)(2,1)S(1)}, bf16[256,4096]{1,0:T(8,128)(2,1)S(1)}, u32[]{:S(2)}, u32[]{:S(2)}) collective-permute-start(bf16[256,4096]{1,0:T(8,128)(2,1)S(1)} %convolution_convert_fusion.1), channel_id=1, source_target_pairs={{0,1},{1,0},{2,3},{3,2},{4,5},{5,4},{6,7},{7,6},{8,9},{9,8},{10,11... | collective-permute-start | bytes 6291464 | tf_op jit(solution)/shard_map/ppermute | solution.py:10
  411.4 28.4 %collective-permute-start.52 = (bf16[144,4096]{1,0:T(8,128)(2,1)S(1)}, bf16[144,4096]{1,0:T(8,128)(2,1)S(1)}, u32[]{:S(2)}, u32[]{:S(2)}) collective-permute-start(bf16[144,4096]{1,0:T(8,128)(2,1)S(1)} %get-tuple-element.70), channel_id=1, source_target_pairs={{0,4},{4,0},{1,5},{5,1},{2,6},{6,2},{3,7},{7,3},{8,12},{12,8},{9,1... | collective-permute-start | bytes 3538952 | tf_op jit(solution)/shard_map/ppermute | solution.py:10
  432.5 22.8 %collective-permute-start.62 = (bf16[128,4096]{1,0:T(8,128)(2,1)S(1)}, bf16[128,4096]{1,0:T(8,128)(2,1)S(1)}, u32[]{:S(2)}, u32[]{:S(2)}) collective-permute-start(bf16[128,4096]{1,0:T(8,128)(2,1)S(1)} %get-tuple-element.84), channel_id=1, source_target_pairs={{0,8},{8,16},{1,9},{9,17},{2,10},{10,18},{3,11},{11,19},{4,12},{12... | collective-permute-start | bytes 3145736 | tf_op jit(solution)/shard_map/ppermute | solution.py:173
  434.0 21.3 %collective-permute-start.65 = (bf16[128,4096]{1,0:T(8,128)(2,1)S(1)}, bf16[128,4096]{1,0:T(8,128)(2,1)S(1)}, u32[]{:S(2)}, u32[]{:S(2)}) collective-permute-start(bf16[128,4096]{1,0:T(8,128)(2,1)S(1)} %get-tuple-element.85), channel_id=1, source_target_pairs={{16,8},{24,16},{17,9},{25,17},{18,10},{26,18},{19,11},{27,19},{20,... | collective-permute-start | bytes 3145736 | tf_op jit(solution)/shard_map/ppermute | solution.py:176
  439.9 24.8 %collective-permute-start.59 = (bf16[128,4096]{1,0:T(8,128)(2,1)S(1)}, bf16[128,4096]{1,0:T(8,128)(2,1)S(1)}, u32[]{:S(2)}, u32[]{:S(2)}) collective-permute-start(bf16[128,4096]{1,0:T(8,128)(2,1)S(1)} %slice.413), channel_id=1, source_target_pairs={{0,2},{2,0},{1,3},{3,1},{4,6},{6,4},{5,7},{7,5},{8,10},{10,8},{9,1... | collective-permute-start | bytes 3145736 | tf_op jit(solution)/shard_map/ppermute | solution.py:10
  442.9 26.2 %collective-permute-start.56 = (bf16[256,4096]{1,0:T(8,128)(2,1)S(1)}, bf16[256,4096]{1,0:T(8,128)(2,1)S(1)}, u32[]{:S(2)}, u32[]{:S(2)}) collective-permute-start(bf16[256,4096]{1,0:T(8,128)(2,1)S(1)} %convolution_convert_fusion), channel_id=1, source_target_pairs={{0,1},{1,0},{2,3},{3,2},{4,5},{5,4},{6,7},{7,6},{8,9},{9,8},{10,11... | collective-permute-start | bytes 6291464 | tf_op jit(solution)/shard_map/ppermute | solution.py:10
  465.6 23.0 %collective-permute-start.63 = (bf16[128,4096]{1,0:T(8,128)(2,1)S(1)}, bf16[128,4096]{1,0:T(8,128)(2,1)S(1)}, u32[]{:S(2)}, u32[]{:S(2)}) collective-permute-start(bf16[128,4096]{1,0:T(8,128)(2,1)S(1)} %get-tuple-element.82), channel_id=1, source_target_pairs={{0,8},{8,16},{16,24},{1,9},{9,17},{17,25},{2,10},{10,18},{18,26},{... | collective-permute-start | bytes 3145736 | tf_op jit(solution)/shard_map/ppermute | solution.py:173
  467.8 25.0 %collective-permute-start.66 = (bf16[128,4096]{1,0:T(8,128)(2,1)S(1)}, bf16[128,4096]{1,0:T(8,128)(2,1)S(1)}, u32[]{:S(2)}, u32[]{:S(2)}) collective-permute-start(bf16[128,4096]{1,0:T(8,128)(2,1)S(1)} %get-tuple-element.83), channel_id=1, source_target_pairs={{8,0},{16,8},{24,16},{9,1},{17,9},{25,17},{10,2},{18,10},{26,18},{... | collective-permute-start | bytes 3145736 | tf_op jit(solution)/shard_map/ppermute | solution.py:176
  471.6 23.1 %collective-permute-start.60 = (bf16[128,4096]{1,0:T(8,128)(2,1)S(1)}, bf16[128,4096]{1,0:T(8,128)(2,1)S(1)}, u32[]{:S(2)}, u32[]{:S(2)}) collective-permute-start(bf16[128,4096]{1,0:T(8,128)(2,1)S(1)} %slice.412), channel_id=1, source_target_pairs={{0,2},{2,0},{1,3},{3,1},{4,6},{6,4},{5,7},{7,5},{8,10},{10,8},{9,1... | collective-permute-start | bytes 3145736 | tf_op jit(solution)/shard_map/ppermute | solution.py:10
  (41 other events, 406.3 us)
